TPU v7x, 128 devices: a whole 4x4x4 slice. The times are simulated.
128 devices in a mesh: node: 16 (over y, z_hi, core), local: 8 (over x, z_lo).
Axes of the slice: x: 4, y: 4, z: 4 (z_hi: 2, z_lo: 2; z = z_hi * 2 + z_lo), core: 2. Of those that a mesh axis runs over, the one named last changes fastest.
Arguments:
- inputs: bfloat16 [2, 8192, 6144], P(None, ('node', 'local')), may hold values from -24 to 24
- weight: bfloat16 [6144, 6144], P('node', 'local'), may hold values from -0.078125 to 0.078125
- cotangent: bfloat16 [2, 8192, 6144], P(None, 'node', 'local'), may hold values from -6 to 6
Outputs:
- output: bfloat16 [2, 8192, 6144], P(None, 'node', 'local')
- input_grad: bfloat16 [2, 8192, 6144], P(None, ('node', 'local'))
- weight_grad: bfloat16 [6144, 6144], P('node', 'local')
All inputs are finite; a program needn't handle non-finite values.
Results may differ from a plain program's by a relative error of at most 0.017.
Values may be sent and summed in bfloat16 or wider, within the bound.
A program may use at most 192 MiB of HBM per device.

v0:
```python
import math

import jax
import jax.numpy as jnp
from jax import lax
from jax.sharding import PartitionSpec as P


def body(inputs, weight, cotangent):
    micro_count = inputs.shape[0]
    whole_weight = lax.all_gather(weight, "node", axis=0, tiled=True)
    in_width, block_cols = whole_weight.shape
    node_count = lax.axis_size("node")
    grad_scale = 1.0 / math.sqrt(
        micro_count * inputs.shape[1] * node_count * lax.axis_size("local")
    )
    outputs = []
    in_grads = []
    gathered = []
    for micro_step in range(micro_count):
        rows = lax.all_gather(inputs[micro_step], "local", axis=0, tiled=True)
        gathered.append(rows)
        outputs.append(
            jnp.dot(rows, whole_weight, preferred_element_type=jnp.float32).astype(jnp.bfloat16)
        )
        partial_value = jnp.einsum(
            "te,de->td", cotangent[micro_step], whole_weight, preferred_element_type=jnp.float32
        )
        in_grads.append(
            lax.psum_scatter(
                partial_value.astype(jnp.bfloat16), "local", scatter_dimension=0, tiled=True
            )
        )
    accum = jnp.zeros((in_width, block_cols), jnp.float32)
    for micro_step in range(micro_count):
        accum = accum + jnp.einsum(
            "td,te->de",
            gathered[micro_step],
            cotangent[micro_step],
            preferred_element_type=jnp.float32,
        )
    weight_grad = lax.psum_scatter(
        (accum * grad_scale).astype(jnp.bfloat16), "node", scatter_dimension=0, tiled=True
    )
    return (jnp.stack(outputs), jnp.stack(in_grads), weight_grad)


def solution(mesh):
    return jax.shard_map(
        body,
        mesh=mesh,
        in_specs=(P(None, ("node", "local"), None), P("node", "local"), P(None, "node", "local")),
        out_specs=(P(None, "node", "local"), P(None, ("node", "local"), None), P("node", "local")),
        check_vma=False,
    )
```

profile of v0, /device:TPU:1, one launch (start us, length us, event | category | flops | bytes accessed | tf_op | source)
XLA Modules:
  0.0 738.2 jit_solution(1752951928449270141)
XLA Ops:
  7.2 0.0 all-gather.6.cloned.1.call-start
  7.2 0.7 all-gather.6.cloned.1.call-update
  7.9 0.0 all-gather.8.cloned.1.call-start
  7.9 2.6 fusion.27
  10.6 0.0 all-gather.8.cloned.1.call-update
  10.6 0.0 all-gather.10.cloned.1.call-start
  10.7 0.7 all-gather.10.cloned.1.call-update
  11.4 0.0 reduce-scatter.4.cloned.1.call-start
  11.4 79.8 %all-gather.6.cloned.1.call-done = bf16[6144,768]{1,0:T(8,128)(2,1)} async-done(((bf16[384,768]{1,0:T(8,128)(2,1)}), bf16[6144,768]{1,0:T(8,128)(2,1)}) %all-gather.6.cloned.1.call-update) | async-done | bytes 9437200 | tf_op jit(solution)/shard_map/all_gather | solution.py:11
  91.3 10.8 %convolution_convert_fusion.1 = bf16[512,6144]{1,0:T(8,128)(2,1)} fusion(bf16[6144,768]{1,0:T(8,128)(2,1)} %all-gather.6.cloned.1.call-done, bf16[2,512,768]{2,1,0:T(8,128)(2,1)} %param.5), kind=kOutput, calls=%fused_computation.2 | convolution fusion | flops 4834983936 | bytes 16515072 | tf_op jit(solution)/shard_map/te,de->td/dot_general | solution.py:26
  102.0 0.0 copy-start
  102.0 0.0 reduce-scatter.4.cloned.1.call-update
  102.1 0.0 reduce-scatter.6.cloned.1.call-start
  102.1 1.3 copy-done
  103.4 10.7 %convolution_convert_fusion = bf16[512,6144]{1,0:T(8,128)(2,1)} fusion(bf16[6144,768]{1,0:T(8,128)(2,1)} %all-gather.6.cloned.1.call-done, bf16[2,512,768]{2,1,0:T(8,128)(2,1)S(1)} %copy-done), kind=kOutput, calls=%fused_computation.1 | convolution fusion | flops 4834983936 | bytes 16515072 | tf_op jit(solution)/shard_map/te,de->td/dot_general | solution.py:26
  114.1 0.0 reduce-scatter.6.cloned.1.call-update
  114.2 0.2 reduce-scatter.8.cloned.1.call-start
  114.4 105.4 %all-gather.8.cloned.1.call-done = bf16[1,512,6144]{2,1,0:T(8,128)(2,1)} async-done(((bf16[1,64,6144]{2,1,0:T(8,128)(2,1)}), bf16[1,512,6144]{2,1,0:T(8,128)(2,1)}) %all-gather.8.cloned.1.call-update) | async-done | bytes 6291472 | tf_op jit(solution)/shard_map/all_gather | solution.py:21
  219.8 11.9 %fusion.3 = f32[6144,768]{1,0:T(8,128)} fusion(bf16[1,512,6144]{2,1,0:T(8,128)(2,1)} %all-gather.8.cloned.1.call-done, bf16[2,512,768]{2,1,0:T(8,128)(2,1)S(1)} %copy-done), kind=kOutput, calls=%fused_computation.6 | convolution fusion | flops 4831838208 | bytes 25952256 | tf_op jit(solution)/shard_map/td,te->de/dot_general | solution.py:36
  231.7 120.9 %all-gather.10.cloned.1.call-done = bf16[1,512,6144]{2,1,0:T(8,128)(2,1)} async-done(((bf16[1,64,6144]{2,1,0:T(8,128)(2,1)}), bf16[1,512,6144]{2,1,0:T(8,128)(2,1)}) %all-gather.10.cloned.1.call-update) | async-done | bytes 6291472 | tf_op jit(solution)/shard_map/all_gather | solution.py:21
  352.6 15.3 %multiply_convert_fusion = bf16[6144,768]{1,0:T(8,128)(2,1)} fusion(f32[6144,768]{1,0:T(8,128)} %fusion.3, bf16[1,512,6144]{2,1,0:T(8,128)(2,1)} %all-gather.10.cloned.1.call-done, bf16[2,512,768]{2,1,0:T(8,128)(2,1)S(1)} %copy-done), kind=kOutput, calls=%fused_computation | convolution fusion | flops 4845993984 | bytes 35389440 | tf_op jit(solution)/shard_map/td,te->de/dot_general | solution.py:36
  367.9 0.0 slice-start
  367.9 0.0 reduce-scatter.8.cloned.1.call-update
  367.9 0.0 slice-start.1
  367.9 0.0 slice-start.2
  367.9 10.0 %fusion.13 = bf16[1,512,768]{2,1,0:T(8,128)(2,1)S(1)} fusion(bf16[6144,768]{1,0:T(8,128)(2,1)} %all-gather.6.cloned.1.call-done, bf16[1,512,6144]{2,1,0:T(8,128)(2,1)} %all-gather.10.cloned.1.call-done), kind=kOutput, calls=%fused_computation.14 | convolution fusion | flops 4832231424 | bytes 16515072 | tf_op jit(solution)/shard_map/dot_general | solution.py:24
  378.0 0.0 slice-done
  378.0 0.0 slice-done.1
  378.0 0.0 slice-done.2
  378.0 7.1 fusion.16
  385.1 1.3 pad_maximum_fusion
  386.4 99.8 %reduce-scatter.4.cloned.1.call-done = bf16[64,6144]{1,0:T(8,128)(2,1)} async-done(((bf16[512,6144]{1,0:T(8,128)(2,1)}), bf16[64,6144]{1,0:T(8,128)(2,1)}) %reduce-scatter.4.cloned.1.call-update) | async-done | bytes 786448 | tf_op jit(solution)/shard_map/reduce_scatter | solution.py:30
  486.2 133.0 %reduce-scatter.6.cloned.1.call-done = bf16[64,6144]{1,0:T(8,128)(2,1)} async-done(((bf16[512,6144]{1,0:T(8,128)(2,1)}), bf16[64,6144]{1,0:T(8,128)(2,1)}) %reduce-scatter.6.cloned.1.call-update) | async-done | bytes 786448 | tf_op jit(solution)/shard_map/reduce_scatter | solution.py:30
  619.2 2.7 pad_maximum_fusion.1
  621.8 109.5 %reduce-scatter.8.cloned.1.call-done = bf16[384,768]{1,0:T(8,128)(2,1)} async-done(((bf16[6144,768]{1,0:T(8,128)(2,1)}), bf16[384,768]{1,0:T(8,128)(2,1)}) %reduce-scatter.8.cloned.1.call-update) | async-done | bytes 589840 | tf_op jit(solution)/shard_map/reduce_scatter | solution.py:42
  (1 shorter events, 0.0 us)
Async XLA Ops:
  7.2 84.1 %all-gather.6.cloned.1.call-start = ((), (), s32[]{:S(2)}) async-start(), calls=%async_computation.3 | async-start | bytes 10027008 | tf_op jit(solution)/shard_map/all_gather | solution.py:11
  7.9 211.9 %all-gather.8.cloned.1.call-start = ((), (), s32[]{:S(2)}) async-start(), calls=%async_computation.7 | async-start | bytes 7077888 | tf_op jit(solution)/shard_map/all_gather | solution.py:21
  10.6 342.0 %all-gather.10.cloned.1.call-start = ((), (), s32[]{:S(2)}) async-start(), calls=%async_computation.8 | async-start | bytes 7077888 | tf_op jit(solution)/shard_map/all_gather | solution.py:21
  11.4 474.8 %reduce-scatter.4.cloned.1.call-start = ((), (), s32[]{:S(2)}) async-start(), calls=%async_computation.4 | async-start | bytes 7077888 | tf_op jit(solution)/shard_map/reduce_scatter | solution.py:30
  102.0 1.4 copy-start
  102.1 517.1 %reduce-scatter.6.cloned.1.call-start = ((), (), s32[]{:S(2)}) async-start(), calls=%async_computation.5 | async-start | bytes 7077888 | tf_op jit(solution)/shard_map/reduce_scatter | solution.py:30
  114.2 617.2 %reduce-scatter.8.cloned.1.call-start = ((), (), s32[]{:S(2)}) async-start(), calls=%async_computation.6 | async-start | bytes 10027008 | tf_op jit(solution)/shard_map/reduce_scatter | solution.py:42
  367.9 10.1 %slice-start = ((s8[9437184]{0:T(1024)(128)(4,1)}), s8[1048576]{0:T(1024)(128)(4,1)S(1)}, s32[]{:S(2)}) async-start(s8[9437184]{0:T(1024)(128)(4,1)} %bitcast.40), calls=%async_computation.9 | async-start | bytes 2097152
  367.9 10.1 %slice-start.1 = ((s8[9437184]{0:T(1024)(128)(4,1)}), s8[4194304]{0:T(1024)(128)(4,1)S(1)}, s32[]{:S(2)}) async-start(s8[9437184]{0:T(1024)(128)(4,1)} %bitcast.40), calls=%async_computation.10 | async-start | bytes 8388608
  367.9 10.1 %slice-start.2 = ((s8[9437184]{0:T(1024)(128)(4,1)}), s8[4194304]{0:T(1024)(128)(4,1)S(1)}, s32[]{:S(2)}) async-start(s8[9437184]{0:T(1024)(128)(4,1)} %bitcast.40), calls=%async_computation.11 | async-start | bytes 8388608
Sparse Core Ops, SparseCore 0:
  10.4 80.8 all-gather.5
  93.5 126.2 all-gather.7
  222.0 130.5 all-gather.9
  354.8 131.2 reduce-scatter.3
  488.4 130.7 reduce-scatter.5
  624.0 107.2 reduce-scatter.7
where the time goes:
time: 739 us; the launch traced here: 738 us
  waiting for transfers between devices  650 us (88%)
  matrix products  65.8 us (9%)
  between operations  14.2 us (2%)
    reduce_scatter x2, waiting for transfers between devices, body(): lax.psum_scatter(partial_value.astype(jnp.bfloat16), 'local', scatter_dim...  233 us
    all_gather x2, waiting for transfers between devices, body(): rows = lax.all_gather(inputs[micro_step], 'local', axis=0, tiled=True)  226 us
    reduce_scatter x1, waiting for transfers between devices, body(): lax.psum_scatter((accum * grad_scale).astype(jnp.bfloat16), 'node', scatt...  110 us
    all_gather x1, waiting for transfers between devices, body(): whole_weight = lax.all_gather(weight, 'node', axis=0, tiled=True)  79.8 us
    dot_general x2, matrix products, body(): jnp.einsum('td,te->de', gathered[micro_step], cotangent[micro_step], pref...  27.2 us
    dot_general x2, matrix products, body(): jnp.einsum('te,de->td', cotangent[micro_step], whole_weight, preferred_el...  21.5 us
    dot_general x2, matrix products, body(): jnp.dot(rows, whole_weight, preferred_element_type=jnp.float32)  17.1 us
  transfers between devices with their start and end apart: 6, of which 6 were waited for; matrix products, arithmetic and copies ran while one was open for 10% of the time, Pallas kernels for 0%

commit v1 on v0

v1 whole, which is shorter than its diff:
```python
import functools
import math

import jax
import jax.numpy as jnp
from jax import lax
from jax.experimental import pallas as pl
from jax.experimental.pallas import tpu as pltpu
from jax.sharding import PartitionSpec as P

MESH = pl.DeviceIdType.MESH
F32 = jnp.float32
BF16 = jnp.bfloat16
NX = 4
ROWS = 64
STRIPE = 384
BLOCK = 768
GROUP = 512
HALF = 3072
WIDE = 1536
UNIT = 768
TILE = 256


def kernel(
    scale, x_ref, w_ref, c_ref, y_out, dx_out, dw_out,
    xg, wg, cg, dxp, fx, nx, dxf, ysend, yrecv, yfin, dws, dwr, dwq, fy, ny, osnd, orcv, dwf,
    xloc, zx_s, zx_r, cloc, c_s, c_r, wloc, wd_s, wd_r, wo_s, wo_r, xr_s, xr_r, yr_s, yr_r, sib_s, sib_r,
    dx_s, dx_r, dxz_s, dxz_r, dxl, yy_s, yy_r, yl, dws_s, dws_r, dy_s, dy_r, do_s, do_r, dd_s, dd_r, ddl,
):
    node, local = lax.axis_index("node"), lax.axis_index("local")
    x, l = local // 2, local % 2
    y, h, c = node // 4, (node // 2) % 2, node % 2
    t = (l + h) % 2
    lw = (c + h) % 2
    keeps = c == t

    def dev(x_, y_, h_, l_, c_):
        return ((y_ * 2 + h_) * 2 + c_, x_ * 2 + l_)

    def up(v, by):
        return lax.rem(v + by + NX, NX)

    zp = dev(x, y, h, 1 - l, c)
    sib = dev(x, y, h, l, 1 - c)
    diag = dev(x, y, h, 1 - l, 1 - c)
    outer = dev(x, y, 1 - h, 1 - l, 1 - c)
    step = (1, -1)
    xn = [dev(up(x, s), y, h, l, c) for s in step]
    yn = [dev(x, up(y, s), h, l, c) for s in step]

    def remote(src, dst, ssem, rsem, to):
        return pltpu.make_async_remote_copy(
            src_ref=src, dst_ref=dst, send_sem=ssem, recv_sem=rsem, device_id=to, device_id_type=MESH
        )

    def at(start, size, multiple):
        return pl.ds(pl.multiple_of(start, multiple), size)

    lo = at(l * BLOCK, BLOCK, BLOCK)
    lz = at((1 - l) * BLOCK, BLOCK, BLOCK)
    lwc = at(lw * BLOCK, BLOCK, BLOCK)
    lwz = at((1 - lw) * BLOCK, BLOCK, BLOCK)

    def x_rows(x_, l_):
        return at(x_ * (2 * ROWS) + l_ * ROWS, ROWS, ROWS)

    def x_local(s):
        return pltpu.make_async_copy(
            x_ref.at[:, :, at((2 * s + t) * STRIPE, STRIPE, STRIPE)],
            xg.at[:, x_rows(x, l), s * STRIPE : (s + 1) * STRIPE],
            xloc.at[s],
        )

    def x_swap(s, l_from):
        return remote(
            x_ref.at[:, :, at((2 * s + 1 - t) * STRIPE, STRIPE, STRIPE)],
            xg.at[:, x_rows(x, l_from), s * STRIPE : (s + 1) * STRIPE],
            zx_s.at[s], zx_r.at[s], zp,
        )

    def x_ring(x_, lrel, d, k):
        micro = d if k != 1 else 1 - d
        owner = x_ if k < 2 else up(x_, -step[d])
        part = xg.at[micro, x_rows(owner, l if lrel == 0 else 1 - l)]
        return remote(part, part, xr_s.at[lrel, d, k], xr_r.at[lrel, d, k], xn[d])

    def stripe(y_, hrel):
        return y_ * 2 + (h if hrel == 0 else 1 - h)

    def w_part(s, cols, piece=None):
        if piece is None:
            return wg.at[at(s * STRIPE, STRIPE, STRIPE), cols]
        return wg.at[at(s * STRIPE + piece * (STRIPE // 2), STRIPE // 2, STRIPE // 2), cols]

    def w_local():
        return pltpu.make_async_copy(w_ref, w_part(stripe(y, 0), lwc), wloc)

    def w_diag(cols):
        return remote(w_ref, w_part(stripe(y, 0), cols), wd_s, wd_r, diag)

    def w_outer(hrel):
        part = w_part(stripe(y, hrel), lwc)
        return remote(part, part, wo_s, wo_r, outer)

    def w_ring(y_, hrel, d, k):
        piece = d if k != 1 else 1 - d
        owner = y_ if k < 2 else up(y_, -step[d])
        part = w_part(stripe(owner, hrel), lwc, piece)
        return remote(part, part, yr_s.at[hrel, d, k], yr_r.at[hrel, d, k], yn[d])

    def w_sib(s, cols):
        part = w_part(s, cols)
        return remote(part, part, sib_s.at[s], sib_r.at[s], sib)

    def c_local():
        return pltpu.make_async_copy(c_ref, cg.at[:, :, lo], cloc)

    def c_swap(cols):
        return remote(c_ref, cg.at[:, :, cols], c_s, c_r, zp)

    def unit_of(i):
        return up(y, i + jnp.where(i == 2, 1, 0) - jnp.where(i == 3, 1, 0))

    def unit_back(i):
        return up(y, jnp.where(i == 0, 2, jnp.where(i == 1, 1, jnp.where(i == 2, 3, 0))))

    def dx_ring(i, d, k):
        ks = at(unit_of(i) * UNIT, UNIT, UNIT)
        micro = d if k != 1 else 1 - d
        to = up(x, 2) if k == 0 else up(x, step[d])
        src = dxp.at[micro, at(to * (2 * ROWS), 2 * ROWS, 2 * ROWS), ks]
        dst = fx.at[d, :, ks] if k == 0 else nx.at[d, micro, :, ks]
        return remote(src, dst, dx_s.at[i, d, k], dx_r.at[i, d, k], xn[d])

    def dx_back(i, e, t_, mine):
        s = unit_of(i) * 2 + e
        rows = at((l if mine else 1 - l) * ROWS, ROWS, ROWS)
        src = dxf.at[:, rows, at(s * STRIPE, STRIPE, STRIPE)]
        dst = dx_out.at[:, :, at((2 * s + t_) * STRIPE, STRIPE, STRIPE)]
        if mine:
            return pltpu.make_async_copy(src, dst, dxl.at[i, e])
        return remote(src, dst, dxz_s.at[i, e], dxz_r.at[i, e], zp)

    def y_swap(m):
        return remote(ysend.at[m], yrecv.at[m], yy_s.at[m], yy_r.at[m], zp)

    def y_store(m):
        return pltpu.make_async_copy(yfin.at[m], y_out.at[m], yl.at[m])

    def dw_sib(i):
        rows = at(unit_back(i) * UNIT, UNIT, UNIT)
        return remote(dws.at[rows], dwr.at[rows], dws_s.at[i], dws_r.at[i], sib)

    def dw_rows(y_, piece):
        return at(y_ * UNIT + piece * STRIPE, STRIPE, STRIPE)

    def dw_ring(d, k):
        piece = d if k != 1 else 1 - d
        to = up(y, 2) if k == 0 else up(y, step[d])
        dst = fy.at[d] if k == 0 else ny.at[d, piece * STRIPE : (piece + 1) * STRIPE]
        return remote(dwq.at[dw_rows(to, piece)], dst, dy_s.at[d, k], dy_r.at[d, k], yn[d])

    def dw_outer():
        return remote(osnd, orcv, do_s, do_r, outer)

    def dw_diag():
        return remote(dwf, dw_out, dd_s, dd_r, diag)

    def dw_local():
        return pltpu.make_async_copy(dwf, dw_out, ddl)

    for s in range(8):
        x_local(s).start()
    c_local().start()

    @pl.when(keeps)
    def _():
        w_local().start()

    barrier = pltpu.get_barrier_semaphore()
    friends = [zp, sib, diag, outer, *xn, *yn]
    for friend in friends:
        pl.semaphore_signal(barrier, inc=1, device_id=friend, device_id_type=MESH)
    pl.semaphore_wait(barrier, len(friends))

    @pl.when(jnp.logical_not(keeps))
    def _():
        w_diag(lo).start()

    for s in range(8):
        x_swap(s, l).start()
    for s in range(8):
        x_local(s).wait()
    for k in (0, 1):
        for d in (0, 1):
            x_ring(x, 0, d, k).start()

    @pl.when(keeps)
    def _():
        w_local().wait()

    @pl.when(jnp.logical_not(keeps))
    def _():
        w_diag(lwc).wait_recv()

    w_outer(0).start()
    for k in (0, 1):
        for d in (0, 1):
            w_ring(y, 0, d, k).start()
    w_sib(stripe(y, 0), lwc).start()

    def x_from(d):
        return up(x, -step[d])

    def y_from(d):
        return up(y, -step[d])

    for d in (0, 1):
        x_ring(x_from(d), 0, d, 0).wait_recv()
        x_ring(x, 0, d, 2).start()
    for d in (0, 1):
        w_ring(y_from(d), 0, d, 0).wait_recv()
        w_ring(y, 0, d, 2).start()
    w_outer(1).wait_recv()
    for k in (0, 1):
        for d in (0, 1):
            w_ring(y, 1, d, k).start()
    w_sib(stripe(y, 1), lwc).start()
    for s in range(8):
        x_swap(s, l).wait_send()
    c_swap(lo).start()
    for s in range(8):
        x_swap(s, 1 - l).wait_recv()
    for k in (0, 1):
        for d in (0, 1):
            x_ring(x, 1, d, k).start()
    for d in (0, 1):
        w_ring(y_from(d), 0, d, 1).wait_recv()
        w_sib(stripe(y_from(d), 0), lwc).start()
    for d in (0, 1):
        w_ring(y_from(d), 0, d, 2).wait_recv()
    w_sib(stripe(up(y, 2), 0), lwc).start()
    for d in (0, 1):
        w_ring(y_from(d), 1, d, 0).wait_recv()
        w_ring(y, 1, d, 2).start()
    for d in (0, 1):
        x_ring(x_from(d), 1, d, 0).wait_recv()
        x_ring(x, 1, d, 2).start()
    for d in (0, 1):
        w_ring(y_from(d), 1, d, 1).wait_recv()
        w_sib(stripe(y_from(d), 1), lwc).start()
    for d in (0, 1):
        w_ring(y_from(d), 1, d, 2).wait_recv()
    w_sib(stripe(up(y, 2), 1), lwc).start()
    for d in (0, 1):
        x_ring(x_from(d), 0, d, 1).wait_recv()
        x_ring(x_from(d), 0, d, 2).wait_recv()
    for s in range(8):
        w_sib(s, lwz).wait_recv()
    for d in (0, 1):
        x_ring(x_from(d), 1, d, 1).wait_recv()
        x_ring(x_from(d), 1, d, 2).wait_recv()

    for m in (0, 1):

        @pl.loop(0, BLOCK // TILE)
        def _(j):
            cols = at((1 - l) * BLOCK + j * TILE, TILE, TILE)
            ysend[m, :, at(j * TILE, TILE, TILE)] = jnp.dot(
                xg[m], wg[:, cols], preferred_element_type=F32
            ).astype(BF16)

        y_swap(m).start()

    c_local().wait()
    c_swap(lz).wait_recv()

    def dx_relay(i):
        ks = at(unit_of(i) * UNIT, UNIT, UNIT)
        for d in (0, 1):
            dx_ring(i, d, 0).wait_recv()
            rows = at(up(x, step[d]) * (2 * ROWS), 2 * ROWS, 2 * ROWS)
            dxp[d, rows, ks] = (dxp[d, rows, ks].astype(F32) + fx[d, :, ks].astype(F32)).astype(BF16)
            dx_ring(i, d, 2).start()

    def dx_final(i):
        ks = at(unit_of(i) * UNIT, UNIT, UNIT)
        for d in (0, 1):
            for k in (1, 2):
                dx_ring(i, d, k).wait_recv()
        mine = at(x * (2 * ROWS), 2 * ROWS, 2 * ROWS)
        for m in (0, 1):
            dxf[m, :, ks] = (
                dxp[m, mine, ks].astype(F32) + nx[0, m, :, ks].astype(F32) + nx[1, m, :, ks].astype(F32)
            ).astype(BF16)
        for e in (0, 1):
            dx_back(i, e, t, False).start()
            dx_back(i, e, t, True).start()

    @pl.loop(0, 4)
    def _(i):
        base = unit_back(i) * UNIT

        @pl.loop(0, UNIT // TILE)
        def _(j):
            ks = at(base + j * TILE, TILE, TILE)
            xt = xg[:, :, ks].reshape(2 * GROUP, TILE).T
            for q, (off, dst) in enumerate((((1 - lw) * BLOCK, dws), (lw * BLOCK, dwq))):
                for n in range(BLOCK // TILE):
                    cv = cg[:, :, at(off + n * TILE, TILE, TILE)].reshape(2 * GROUP, TILE)
                    acc = jnp.dot(xt, cv, preferred_element_type=F32)
                    dst[ks, n * TILE : (n + 1) * TILE] = (acc * scale).astype(BF16)

        dw_sib(i).start()

        @pl.loop(0, UNIT // TILE)
        def _(j):
            ks = at(unit_of(i) * UNIT + j * TILE, TILE, TILE)
            acc = lax.dot_general(
                cg[...].reshape(2 * GROUP, WIDE), wg[ks, :], (((1,), (1,)), ((), ())),
                preferred_element_type=F32,
            )
            dxp[:, :, ks] = acc.astype(BF16).reshape(2, GROUP, TILE)

        for k in (0, 1):
            for d in (0, 1):
                dx_ring(i, d, k).start()

        dw_sib(i).wait_recv()

        @pl.loop(0, 4)
        def _(j):
            part = at(base + j * (UNIT // 4), UNIT // 4, UNIT // 4)
            dwq[part, :] = (dwq[part, :].astype(F32) + dwr[part, :].astype(F32)).astype(BF16)

        @pl.when(i == 0)
        def _():
            dw_ring(0, 0).start()
            dw_ring(1, 0).start()

        @pl.when(i == 1)
        def _():
            dw_ring(0, 1).start()

        @pl.when(i == 2)
        def _():
            dw_ring(1, 1).start()

        @pl.when(i > 0)
        def _():
            dx_relay(i - 1)

    for d in (0, 1):
        dw_ring(d, 0).wait_recv()
        rows = dw_rows(up(y, step[d]), d)
        dwq[rows, :] = (dwq[rows, :].astype(F32) + fy[d].astype(F32)).astype(BF16)
        dw_ring(d, 2).start()
    dx_relay(3)
    dx_final(0)

    for m in (0, 1):
        y_swap(m).wait_recv()

        @pl.loop(0, BLOCK // TILE)
        def _(j):
            cols = at(l * BLOCK + j * TILE, TILE, TILE)
            js = at(j * TILE, TILE, TILE)
            acc = jnp.dot(xg[m], wg[:, cols], preferred_element_type=F32)
            yfin[m, :, js] = (acc + yrecv[m, :, js].astype(F32)).astype(BF16)

        y_store(m).start()

    dx_final(1)
    for d in (0, 1):
        for k in (1, 2):
            dw_ring(d, k).wait_recv()

    def dw_total(h_):
        rows = at(h_ * STRIPE, STRIPE, STRIPE)
        return dwq[dw_rows(y, h_), :].astype(F32) + ny[0, rows, :].astype(F32) + ny[1, rows, :].astype(F32)

    osnd[...] = dw_total(1 - h).astype(BF16)
    dw_outer().start()
    dx_final(2)
    dx_final(3)
    dw_outer().wait_recv()
    dwf[...] = (dw_total(h) + orcv[...].astype(F32)).astype(BF16)

    @pl.when(keeps)
    def _():
        dw_local().start()
        dw_local().wait()

    @pl.when(jnp.logical_not(keeps))
    def _():
        dw_diag().start()
        dw_diag().wait()
        w_diag(lo).wait_send()

    for s in range(8):
        w_sib(s, lwc).wait_send()
    w_outer(0).wait_send()
    c_swap(lo).wait_send()
    for rel in (0, 1):
        for d in (0, 1):
            for k in range(3):
                x_ring(x, rel, d, k).wait_send()
                w_ring(y, rel, d, k).wait_send()
    for d in (0, 1):
        for k in range(3):
            dw_ring(d, k).wait_send()
    dw_outer().wait_send()
    for m in (0, 1):
        y_swap(m).wait_send()
        y_store(m).wait()

    @pl.loop(0, 4)
    def _(i):
        dw_sib(i).wait_send()
        for d in (0, 1):
            for k in range(3):
                dx_ring(i, d, k).wait_send()
        for e in (0, 1):
            dx_back(i, e, t, False).wait_send()
            dx_back(i, e, 1 - t, False).wait_recv()
            dx_back(i, e, t, True).wait()


def body(inputs, weight, cotangent):
    scale = 1.0 / math.sqrt(
        inputs.shape[0] * inputs.shape[1] * lax.axis_size("node") * lax.axis_size("local")
    )
    dma = pltpu.SemaphoreType.DMA
    vmem = [
        (2, GROUP, HALF), (HALF, WIDE), (2, GROUP, WIDE),
        (2, GROUP, HALF), (2, 2 * ROWS, HALF), (2, 2, 2 * ROWS, HALF), (2, 2 * ROWS, HALF),
        (2, GROUP, BLOCK), (2, GROUP, BLOCK), (2, GROUP, BLOCK),
        (HALF, BLOCK), (HALF, BLOCK), (HALF, BLOCK),
        (2, STRIPE, BLOCK), (2, UNIT, BLOCK), (STRIPE, BLOCK), (STRIPE, BLOCK), (STRIPE, BLOCK),
    ]
    sems = [
        (8,), (8,), (8,), (), (), (), (), (), (), (), (), (2, 2, 3), (2, 2, 3), (2, 2, 3), (2, 2, 3), (8,), (8,),
        (4, 2, 3), (4, 2, 3), (4, 2), (4, 2), (4, 2), (2,), (2,), (2,), (4,), (4,), (2, 3), (2, 3), (), (), (), (), (),
    ]
    out = [
        jax.ShapeDtypeStruct((2, GROUP, BLOCK), BF16),
        jax.ShapeDtypeStruct((2, ROWS, 2 * HALF), BF16),
        jax.ShapeDtypeStruct((STRIPE, BLOCK), BF16),
    ]
    return pl.pallas_call(
        functools.partial(kernel, scale),
        out_shape=out,
        in_specs=[pl.BlockSpec(memory_space=pl.ANY)] * 3,
        out_specs=[pl.BlockSpec(memory_space=pl.ANY)] * 3,
        scratch_shapes=[pltpu.VMEM(s, BF16) for s in vmem] + [dma(s) if s else dma for s in sems],
        compiler_params=pltpu.CompilerParams(
            collective_id=0, has_side_effects=True, vmem_limit_bytes=62 * 2**20
        ),
        cost_estimate=pl.CostEstimate(flops=29 * 10**9, bytes_accessed=8 * 2**20, transcendentals=0),
    )(inputs, weight, cotangent)


def solution(mesh):
    return jax.shard_map(
        body,
        mesh=mesh,
        in_specs=(P(None, ("node", "local"), None), P("node", "local"), P(None, "node", "local")),
        out_specs=(P(None, "node", "local"), P(None, ("node", "local"), None), P("node", "local")),
        check_vma=False,
    )
```

time: 739 us -> 150 us (0.20)
  waiting for transfers between devices: 650 us -> 0 us
  Pallas kernels: 0 us -> 144 us
  matrix products: 65.8 us -> 0 us
  between operations: 14.2 us -> 0.65 us
    reduce_scatter x3 -> x0, waiting for transfers between devices: 342 us -> none  [the longest x2 233 us: body(): lax.psum_scatter(partial_value.astype(jnp.bfloat16), 'local', scatter_dim...]
    all_gather x3 -> x0, waiting for transfers between devices: 306 us -> none  [the longest x2 226 us: body(): rows = lax.all_gather(inputs[micro_step], 'local', axis=0, tiled=True)]
    pallas_call x0 -> x1, Pallas kernels: none -> 144 us  [body(): pl.pallas_call(functools.partial(kernel, scale), out_shape=out, in_specs=...]
    dot_general x6 -> x0, matrix products: 65.8 us -> none  [the longest x2 27.2 us: body(): jnp.einsum('td,te->de', gathered[micro_step], cotangent[micro_step], pref...]
  transfers between devices with their start and end apart: 6 -> 0, of which waited for: 6 -> 0; matrix products, arithmetic and copies ran while one was open for 10% -> 0% of each run, Pallas kernels for 0% -> 0%
where the time goes in v1:
time: 150 us
  Pallas kernels  144 us (96%)
  local copies, waits for them, and re-layouts  5.05 us (3%)
    pallas_call x1, Pallas kernels, body(): pl.pallas_call(functools.partial(kernel, scale), out_shape=out, in_specs=...  144 us
    unnamed x7, local copies, waits for them, and re-layouts  5.05 us

profile of v1, /device:TPU:1, one launch (start us, length us, event | category | flops | bytes accessed | tf_op | source)
XLA Modules:
  0.0 149.8 jit_solution(13352450167661804415)
XLA Ops:
  0.6 144.1 %shard_map.58 = (bf16[2,512,768]{2,1,0:T(8,128)(2,1)}, bf16[2,64,6144]{2,1,0:T(8,128)(2,1)}, bf16[384,768]{1,0:T(8,128)(2,1)}) custom-call(bf16[2,64,6144]{2,1,0:T(8,128)(2,1)} %x_ref.1, bf16[384,768]{1,0:T(8,128)(2,1)} %w_ref.1, bf16[2,512,768]{2,1,0:T(8,128)(2,1)} %c_ref.1), custom_call_target="tpu_custom_call" | custom-call | flops 28999999488 | bytes 8388608 | tf_op jit(solution)/shard_map/pallas_call | solution.py:451
  144.7 0.0 copy-start
  144.8 2.8 %copy.9 = bf16[2,512,768]{2,1,0:T(8,128)(2,1)} copy(bf16[2,512,768]{2,1,0:T(8,128)(2,1)} %get-tuple-element.6) | data formatting | bytes 3145728
  147.5 0.0 copy-done
  147.5 0.0 copy-start.1
  147.5 1.1 copy.10
  148.7 0.3 copy-done.1
  149.0 0.8 copy.11
Async XLA Ops:
  144.7 2.8 %copy-start = (bf16[2,64,6144]{2,1,0:T(8,128)(2,1)S(1)}, bf16[2,64,6144]{2,1,0:T(8,128)(2,1)}, u32[]{:S(2)}) copy-start(bf16[2,64,6144]{2,1,0:T(8,128)(2,1)} %get-tuple-element.7) | copy-start | bytes 4718596
  147.5 1.5 copy-start.1

commit v2 on v0

v2 whole, which is shorter than its diff:
```python
import functools
import math

import jax
import jax.numpy as jnp
from jax import lax
from jax.experimental import pallas as pl
from jax.experimental.pallas import tpu as pltpu
from jax.sharding import PartitionSpec as P

MESH = pl.DeviceIdType.MESH
F32 = jnp.float32
BF16 = jnp.bfloat16
NX = 4
ROWS = 64
STRIPE = 384
BLOCK = 768
GROUP = 512
HALF = 3072
WIDE = 1536
UNIT = 768
TILE = 256
FAR, BEFORE, OWN, AFTER = range(4)


def kernel(
    scale, x_ref, w_ref, c_ref, y_out, dx_out, dw_out,
    xg, wg, cg, dxp, fx, nx, dxf, ysend, yrecv, yfin, dwp, dwr, fy, ny, osnd, orcv, dwf,
    xloc, zx_s, zx_r, cloc, c_s, c_r, wloc, wd_s, wd_r, wo_s, wo_r, xr_s, xr_r, yr_s, yr_r, sib_s, sib_r,
    dx_s, dx_r, dxz_s, dxz_r, dxl, yy_s, yy_r, yl, dws_s, dws_r, dy_s, dy_r, do_s, do_r, dd_s, dd_r, ddl,
):
    node, local = lax.axis_index("node"), lax.axis_index("local")
    x, l = local // 2, local % 2
    y, h, c = node // 4, (node // 2) % 2, node % 2
    t = (l + h) % 2
    lw = (c + h) % 2
    keeps = c == t
    mine = jnp.where(keeps, 0, 1)

    def dev(x_, y_, h_, l_, c_):
        return ((y_ * 2 + h_) * 2 + c_, x_ * 2 + l_)

    def turn(v, by):
        return lax.rem(v + by + NX, NX)

    zp = dev(x, y, h, 1 - l, c)
    sib = dev(x, y, h, l, 1 - c)
    diag = dev(x, y, h, 1 - l, 1 - c)
    outer = dev(x, y, 1 - h, 1 - l, 1 - c)
    step = (1, -1)
    xn = [dev(turn(x, s), y, h, l, c) for s in step]
    yn = [dev(x, turn(y, s), h, l, c) for s in step]

    def remote(src, dst, ssem, rsem, to):
        return pltpu.make_async_remote_copy(
            src_ref=src, dst_ref=dst, send_sem=ssem, recv_sem=rsem, device_id=to, device_id_type=MESH
        )

    def at(start, size):
        return pl.ds(pl.multiple_of(start, size), size)

    def half(q):
        return slice(q * STRIPE, (q + 1) * STRIPE)

    lo = at(l * BLOCK, BLOCK)
    lz = at((1 - l) * BLOCK, BLOCK)
    lwc = at(lw * BLOCK, BLOCK)
    lwz = at((1 - lw) * BLOCK, BLOCK)

    def before(d):
        return BEFORE if d == 0 else AFTER

    def ahead(d):
        return AFTER if d == 0 else BEFORE

    def piece(d, k):
        return d if k != 1 else 1 - d

    def own_rows(rel):
        return at((l if rel == 0 else 1 - l) * ROWS, ROWS)

    def columns(v, e):
        return slice(v * UNIT + e * STRIPE, v * UNIT + (e + 1) * STRIPE)

    def stripe_columns(v, e, t_):
        return at(((turn(y, v - OWN) * 2 + e) * 2 + t_) * STRIPE, STRIPE)

    def x_local(v, e):
        return pltpu.make_async_copy(
            x_ref.at[:, :, stripe_columns(v, e, t)], xg.at[:, OWN, own_rows(0), columns(v, e)], xloc.at[v, e]
        )

    def x_swap(v, e, rel):
        return remote(
            x_ref.at[:, :, stripe_columns(v, e, 1 - t)], xg.at[:, OWN, own_rows(rel), columns(v, e)],
            zx_s.at[v, e], zx_r.at[v, e], zp,
        )

    def x_ring(rel, d, k):
        src, dst = (OWN, before(d)) if k < 2 else (before(d), FAR)
        m = piece(d, k)
        return remote(
            xg.at[m, src, own_rows(rel)], xg.at[m, dst, own_rows(rel)],
            xr_s.at[rel, d, k], xr_r.at[rel, d, k], xn[d],
        )

    def e_of(rel):
        return h if rel == 0 else 1 - h

    def w_part(v, e, cols):
        return wg.at[at(v * UNIT + e * STRIPE, STRIPE), cols]

    def w_local():
        return pltpu.make_async_copy(w_ref, w_part(OWN, h, lwc), wloc)

    def w_diag(cols):
        return remote(w_ref, w_part(OWN, h, cols), wd_s, wd_r, diag)

    def w_outer(rel):
        part = w_part(OWN, e_of(rel), lwc)
        return remote(part, part, wo_s, wo_r, outer)

    def w_ring(rel, d, k):
        src, dst = (OWN, before(d)) if k < 2 else (before(d), FAR)
        src, dst = [
            wg.at[at(v * UNIT + e_of(rel) * STRIPE + piece(d, k) * (STRIPE // 2), STRIPE // 2), lwc] for v in (src, dst)
        ]
        return remote(src, dst, yr_s.at[rel, d, k], yr_r.at[rel, d, k], yn[d])

    def w_sib(v, rel, cols):
        part = w_part(v, e_of(rel), cols)
        return remote(part, part, sib_s.at[v, rel], sib_r.at[v, rel], sib)

    def c_rows(s):
        return c_ref.at[:, at(turn(x, s - OWN) * (2 * ROWS), 2 * ROWS)]

    def c_local(s):
        return pltpu.make_async_copy(c_rows(s), cg.at[:, s, :, lo], cloc.at[s])

    def c_swap(s, cols):
        return remote(c_rows(s), cg.at[:, s, :, cols], c_s.at[s], c_r.at[s], zp)

    def dx_ring(v, d, k):
        ks = at(v * UNIT, UNIT)
        m = piece(d, k)
        src = dxp.at[m, FAR if k == 0 else ahead(d), :, ks]
        dst = fx.at[d, :, ks] if k == 0 else nx.at[d, m, :, ks]
        return remote(src, dst, dx_s.at[v, d, k], dx_r.at[v, d, k], xn[d])

    def dx_back(v, e, t_, mine):
        src = dxf.at[:, own_rows(0 if mine else 1), at(v * UNIT + e * STRIPE, STRIPE)]
        dst = dx_out.at[:, :, stripe_columns(v, e, t_)]
        if mine:
            return pltpu.make_async_copy(src, dst, dxl.at[v, e])
        return remote(src, dst, dxz_s.at[v, e], dxz_r.at[v, e], zp)

    def y_swap(m):
        return remote(ysend.at[m], yrecv.at[m], yy_s.at[m], yy_r.at[m], zp)

    def y_store(m, s):
        return pltpu.make_async_copy(
            yfin.at[m, s], y_out.at[m, at(turn(x, s - OWN) * (2 * ROWS), 2 * ROWS)], yl.at[m, s]
        )

    def dw_sib(v):
        rows = at(v * UNIT, UNIT)
        return remote(dwp.at[1, rows], dwr.at[rows], dws_s.at[v], dws_r.at[v], sib)

    def dw_rows(v, e):
        return at(v * UNIT + e * STRIPE, STRIPE)

    def dw_ring(d, k, q):
        p = piece(d, k)
        src = dwp.at[0, dw_rows(FAR if k == 0 else ahead(d), p), half(q)]
        dst = fy.at[d, :, half(q)] if k == 0 else ny.at[d, half(p), half(q)]
        return remote(src, dst, dy_s.at[d, k, q], dy_r.at[d, k, q], yn[d])

    def dw_outer(q):
        return remote(osnd.at[:, half(q)], orcv.at[:, half(q)], do_s.at[q], do_r.at[q], outer)

    def dw_diag(q):
        return remote(dwf.at[:, half(q)], dw_out.at[:, half(q)], dd_s.at[q], dd_r.at[q], diag)

    def dw_local(q):
        return pltpu.make_async_copy(dwf.at[:, half(q)], dw_out.at[:, half(q)], ddl.at[q])

    def y_tile(m, off, j):
        cols = at(off * BLOCK + j * TILE, TILE)
        return jnp.dot(xg[m].reshape(GROUP, HALF), wg[:, cols], preferred_element_type=F32).reshape(4, 2 * ROWS, TILE)

    def dx_rows(v, slots):
        count = slots.stop - slots.start

        @pl.loop(0, UNIT // TILE)
        def _(j):
            ks = at(v * UNIT + j * TILE, TILE)
            acc = lax.dot_general(
                cg[:, slots].reshape(2 * count * 2 * ROWS, WIDE), wg[ks, :], (((1,), (1,)), ((), ())),
                preferred_element_type=F32,
            )
            dxp[:, slots, :, ks] = acc.astype(BF16).reshape(2, count, 2 * ROWS, TILE)

    def dx_far(v):
        dx_rows(v, slice(0, 1))

    def dx_near(v):
        dx_rows(v, slice(1, 4))
        for d in (0, 1):
            dx_ring(v, d, 1).start()

    def dx_relay(v):
        ks = at(v * UNIT, UNIT)
        for d in (0, 1):
            dx_ring(v, d, 0).wait_recv()
            dxp[d, ahead(d), :, ks] = (dxp[d, ahead(d), :, ks].astype(F32) + fx[d, :, ks].astype(F32)).astype(BF16)
            dx_ring(v, d, 2).start()

    def dx_final(v):
        ks = at(v * UNIT, UNIT)
        for k in (1, 2):
            for d in (0, 1):
                dx_ring(v, d, k).wait_recv()
        for m in (0, 1):
            dxf[m, :, ks] = (
                dxp[m, OWN, :, ks].astype(F32) + nx[0, m, :, ks].astype(F32) + nx[1, m, :, ks].astype(F32)
            ).astype(BF16)
        for e in (0, 1):
            dx_back(v, e, t, False).start()
            dx_back(v, e, t, True).start()

    def dw_block(v, own):
        off = (l if own else 1 - l) * BLOCK
        slot = mine if own else 1 - mine

        @pl.loop(0, UNIT // TILE)
        def _(j):
            ks = at(v * UNIT + j * TILE, TILE)
            xt = xg[:, :, :, ks].reshape(2 * GROUP, TILE).T
            for n in range(BLOCK // TILE):
                cv = cg[:, :, :, at(off + n * TILE, TILE)].reshape(2 * GROUP, TILE)
                acc = jnp.dot(xt, cv, preferred_element_type=F32)
                dwp[slot, ks, n * TILE : (n + 1) * TILE] = (acc * scale).astype(BF16)

        @pl.when(jnp.logical_not(keeps) if own else keeps)
        def _():
            dw_sib(v).start()

    def dw_merge(v):
        dw_sib(v).wait_recv()

        @pl.loop(0, 4)
        def _(j):
            part = at(v * UNIT + j * (UNIT // 4), UNIT // 4)
            dwp[0, part, :] = (dwp[0, part, :].astype(F32) + dwr[part, :].astype(F32)).astype(BF16)

    def dw_send_far():
        for q in (0, 1):
            for d in (0, 1):
                dw_ring(d, 0, q).start()

    def dw_send_near(d):
        for q in (0, 1):
            dw_ring(d, 1, q).start()

    def dw_relay(q):
        for d in (0, 1):
            dw_ring(d, 0, q).wait_recv()
            rows = dw_rows(ahead(d), d)
            dwp[0, rows, half(q)] = (dwp[0, rows, half(q)].astype(F32) + fy[d, :, half(q)].astype(F32)).astype(BF16)
            dw_ring(d, 2, q).start()

    def dw_total(e, q):
        rows = at(e * STRIPE, STRIPE)
        return (
            dwp[0, dw_rows(OWN, e), half(q)].astype(F32)
            + ny[0, rows, half(q)].astype(F32)
            + ny[1, rows, half(q)].astype(F32)
        )

    stripes = [(v, e) for v in range(4) for e in range(2)]
    both = (0, 1)
    for v, e in stripes:
        x_local(v, e).start()
    for s in range(4):
        c_local(s).start()

    @pl.when(keeps)
    def _():
        w_local().start()

    barrier = pltpu.get_barrier_semaphore()
    friends = [zp, sib, diag, outer, *xn, *yn]
    for friend in friends:
        pl.semaphore_signal(barrier, inc=1, device_id=friend, device_id_type=MESH)
    pl.semaphore_wait(barrier, len(friends))

    @pl.when(jnp.logical_not(keeps))
    def _():
        w_diag(lo).start()

    @pl.when(keeps)
    def _():
        for v, e in stripes:
            x_swap(v, e, 0).start()

    for v, e in stripes:
        x_local(v, e).wait()
    for k in both:
        for d in both:
            x_ring(0, d, k).start()

    @pl.when(keeps)
    def _():
        w_local().wait()

    @pl.when(jnp.logical_not(keeps))
    def _():
        w_diag(lo).wait_send()
        for v, e in stripes:
            x_swap(v, e, 0).start()
        w_diag(lwc).wait_recv()

    w_outer(0).start()
    for k in both:
        for d in both:
            w_ring(0, d, k).start()
    w_sib(OWN, 0, lwc).start()

    for d in both:
        x_ring(0, d, 0).wait_recv()
        x_ring(0, d, 2).start()
    for d in both:
        w_ring(0, d, 0).wait_recv()
        w_ring(0, d, 2).start()
    w_outer(1).wait_recv()
    for k in both:
        for d in both:
            w_ring(1, d, k).start()
    w_sib(OWN, 1, lwc).start()
    for v, e in stripes:
        x_swap(v, e, 0).wait_send()
    c_swap(FAR, lo).start()
    for v, e in stripes:
        x_swap(v, e, 1).wait_recv()
    for k in both:
        for d in both:
            x_ring(1, d, k).start()
    for d in both:
        w_ring(0, d, 1).wait_recv()
        w_sib(before(d), 0, lwc).start()
    for d in both:
        w_ring(0, d, 2).wait_recv()
    w_sib(FAR, 0, lwc).start()
    c_swap(FAR, lo).wait_send()
    for s in (AFTER, BEFORE, OWN):
        c_swap(s, lo).start()
    for d in both:
        w_ring(1, d, 0).wait_recv()
        w_ring(1, d, 2).start()
    for d in both:
        x_ring(1, d, 0).wait_recv()
        x_ring(1, d, 2).start()
    for d in both:
        w_ring(1, d, 1).wait_recv()
        w_sib(before(d), 1, lwc).start()

    def w_arrived(v):
        for rel in both:
            w_sib(v, rel, lwz).wait_recv()

    for s in (FAR, AFTER, BEFORE, OWN):
        c_local(s).wait()
    c_swap(FAR, lz).wait_recv()
    w_arrived(OWN)
    dx_far(OWN)
    for v in (AFTER, BEFORE):
        w_arrived(v)
        dx_far(v)
    for d in both:
        w_ring(1, d, 2).wait_recv()
    w_sib(FAR, 1, lwc).start()
    w_arrived(FAR)
    dx_far(FAR)
    for rel in both:
        for d in both:
            for k in (1, 2):
                x_ring(rel, d, k).wait_recv()
    for v in (OWN, AFTER, BEFORE, FAR):
        for d in both:
            dx_ring(v, d, 0).start()

    def y_first(m):
        @pl.loop(0, BLOCK // TILE)
        def _(j):
            ysend[m, :, :, at(j * TILE, TILE)] = y_tile(m, 1 - l, j).astype(BF16)

        y_swap(m).start()

    dw_block(FAR, True)
    y_first(0)
    dw_block(AFTER, True)

    @pl.when(keeps)
    def _():
        dw_merge(FAR)
        dw_send_far()

    dw_block(BEFORE, True)

    @pl.when(keeps)
    def _():
        dw_merge(AFTER)
        dw_send_near(0)

    y_first(1)

    @pl.when(keeps)
    def _():
        dw_merge(BEFORE)
        dw_send_near(1)

    dw_block(OWN, True)

    @pl.when(keeps)
    def _():
        dw_merge(OWN)

    for s in (AFTER, BEFORE, OWN):
        c_swap(s, lz).wait_recv()

    def pick(i, a, b, c_, d_):
        return jnp.where(i == 0, a, jnp.where(i == 1, b, jnp.where(i == 2, c_, d_)))

    def dx_order(i):
        return pick(i, OWN, AFTER, BEFORE, FAR)

    def dw_order(i):
        return pick(i, FAR, AFTER, BEFORE, OWN)

    @pl.loop(0, 4)
    def _(i):
        dw_block(dw_order(i), False)
        dx_near(dx_order(i))

        @pl.when(jnp.logical_not(keeps))
        def _():
            dw_merge(dw_order(i))

            @pl.when(i == 0)
            def _():
                dw_send_far()

            @pl.when(i == 1)
            def _():
                dw_send_near(0)

            @pl.when(i == 2)
            def _():
                dw_send_near(1)

        @pl.when(jnp.where(keeps, 0, 2) == i)
        def _():
            for q in both:
                dw_relay(q)

        dx_relay(dx_order(i))

    dx_final(OWN)
    for m in both:
        y_swap(m).wait_recv()

        @pl.loop(0, BLOCK // TILE)
        def _(j):
            js = at(j * TILE, TILE)
            yfin[m, :, :, js] = (y_tile(m, l, j) + yrecv[m, :, :, js].astype(F32)).astype(BF16)

        for s in range(4):
            y_store(m, s).start()

    dx_final(AFTER)
    for q in both:
        for d in both:
            for k in (1, 2):
                dw_ring(d, k, q).wait_recv()
        osnd[:, half(q)] = dw_total(1 - h, q).astype(BF16)
        dw_outer(q).start()
    dx_final(BEFORE)
    dx_final(FAR)
    for q in both:
        dw_outer(q).wait_recv()
        dwf[:, half(q)] = (dw_total(h, q) + orcv[:, half(q)].astype(F32)).astype(BF16)

        @pl.when(keeps)
        def _():
            dw_local(q).start()

        @pl.when(jnp.logical_not(keeps))
        def _():
            dw_diag(q).start()

    for q in both:

        @pl.when(keeps)
        def _():
            dw_local(q).wait()

        @pl.when(jnp.logical_not(keeps))
        def _():
            dw_diag(q).wait()

    for v in range(4):
        for rel in both:
            w_sib(v, rel, lwc).wait_send()
    w_outer(0).wait_send()
    for s in (AFTER, BEFORE, OWN):
        c_swap(s, lo).wait_send()
    for rel in both:
        for d in both:
            for k in range(3):
                x_ring(rel, d, k).wait_send()
                w_ring(rel, d, k).wait_send()
    for q in both:
        for d in both:
            for k in range(3):
                dw_ring(d, k, q).wait_send()
        dw_outer(q).wait_send()
    for m in both:
        y_swap(m).wait_send()
        for s in range(4):
            y_store(m, s).wait()

    @pl.loop(0, 4)
    def _(v):
        dw_sib(v).wait_send()
        for d in both:
            for k in range(3):
                dx_ring(v, d, k).wait_send()
        for e in both:
            dx_back(v, e, t, False).wait_send()
            dx_back(v, e, 1 - t, False).wait_recv()
            dx_back(v, e, t, True).wait()


def body(inputs, weight, cotangent):
    scale = 1.0 / math.sqrt(
        inputs.shape[0] * inputs.shape[1] * lax.axis_size("node") * lax.axis_size("local")
    )
    dma = pltpu.SemaphoreType.DMA
    vmem = [
        (2, 4, 2 * ROWS, HALF), (HALF, WIDE), (2, 4, 2 * ROWS, WIDE),
        (2, 4, 2 * ROWS, HALF), (2, 2 * ROWS, HALF), (2, 2, 2 * ROWS, HALF), (2, 2 * ROWS, HALF),
        (2, 4, 2 * ROWS, BLOCK), (2, 4, 2 * ROWS, BLOCK), (2, 4, 2 * ROWS, BLOCK),
        (2, HALF, BLOCK), (HALF, BLOCK),
        (2, STRIPE, BLOCK), (2, UNIT, BLOCK), (STRIPE, BLOCK), (STRIPE, BLOCK), (STRIPE, BLOCK),
    ]
    sems = [
        (4, 2), (4, 2), (4, 2), (4,), (4,), (4,), (), (), (), (), (), (2, 2, 3), (2, 2, 3), (2, 2, 3), (2, 2, 3), (4, 2), (4, 2),
        (4, 2, 3), (4, 2, 3), (4, 2), (4, 2), (4, 2), (2,), (2,), (2, 4), (4,), (4,), (2, 3, 2), (2, 3, 2), (2,), (2,),
        (2,), (2,), (2,),
    ]
    out = [
        jax.ShapeDtypeStruct((2, GROUP, BLOCK), BF16),
        jax.ShapeDtypeStruct((2, ROWS, 2 * HALF), BF16),
        jax.ShapeDtypeStruct((STRIPE, BLOCK), BF16),
    ]
    return pl.pallas_call(
        functools.partial(kernel, scale),
        out_shape=out,
        in_specs=[pl.BlockSpec(memory_space=pl.ANY)] * 3,
        out_specs=[pl.BlockSpec(memory_space=pl.ANY)] * 3,
        scratch_shapes=[pltpu.VMEM(s, BF16) for s in vmem] + [dma(s) if s else dma for s in sems],
        compiler_params=pltpu.CompilerParams(
            collective_id=0, has_side_effects=True, vmem_limit_bytes=62 * 2**20
        ),
        cost_estimate=pl.CostEstimate(flops=29 * 10**9, bytes_accessed=8 * 2**20, transcendentals=0),
    )(inputs, weight, cotangent)


def solution(mesh):
    return jax.shard_map(
        body,
        mesh=mesh,
        in_specs=(P(None, ("node", "local"), None), P("node", "local"), P(None, "node", "local")),
        out_specs=(P(None, "node", "local"), P(None, ("node", "local"), None), P("node", "local")),
        check_vma=False,
    )
```

time: 739 us -> 134 us (0.18)
  waiting for transfers between devices: 650 us -> 0 us
  Pallas kernels: 0 us -> 128 us
  matrix products: 65.8 us -> 0 us
  between operations: 14.2 us -> 0.65 us
    reduce_scatter x3 -> x0, waiting for transfers between devices: 342 us -> none  [the longest x2 233 us: body(): lax.psum_scatter(partial_value.astype(jnp.bfloat16), 'local', scatter_dim...]
    all_gather x3 -> x0, waiting for transfers between devices: 306 us -> none  [the longest x2 226 us: body(): rows = lax.all_gather(inputs[micro_step], 'local', axis=0, tiled=True)]
    pallas_call x0 -> x1, Pallas kernels: none -> 128 us  [body(): pl.pallas_call(functools.partial(kernel, scale), out_shape=out, in_specs=...]
    dot_general x6 -> x0, matrix products: 65.8 us -> none  [the longest x2 27.2 us: body(): jnp.einsum('td,te->de', gathered[micro_step], cotangent[micro_step], pref...]
  transfers between devices with their start and end apart: 6 -> 0, of which waited for: 6 -> 0; matrix products, arithmetic and copies ran while one was open for 10% -> 0% of each run, Pallas kernels for 0% -> 0%
where the time goes in v2:
time: 134 us
  Pallas kernels  128 us (96%)
  local copies, waits for them, and re-layouts  5.05 us (4%)
    pallas_call x1, Pallas kernels, body(): pl.pallas_call(functools.partial(kernel, scale), out_shape=out, in_specs=...  128 us
    unnamed x7, local copies, waits for them, and re-layouts  5.05 us

profile of v2, /device:TPU:1, one launch (start us, length us, event | category | flops | bytes accessed | tf_op | source)
XLA Modules:
  0.0 134.1 jit_solution(3219821606480140009)
XLA Ops:
  0.6 128.4 %shard_map.58 = (bf16[2,512,768]{2,1,0:T(8,128)(2,1)}, bf16[2,64,6144]{2,1,0:T(8,128)(2,1)}, bf16[384,768]{1,0:T(8,128)(2,1)}) custom-call(bf16[2,64,6144]{2,1,0:T(8,128)(2,1)} %x_ref.1, bf16[384,768]{1,0:T(8,128)(2,1)} %w_ref.1, bf16[2,512,768]{2,1,0:T(8,128)(2,1)} %c_ref.1), custom_call_target="tpu_custom_call" | custom-call | flops 28999999488 | bytes 8388608 | tf_op jit(solution)/shard_map/pallas_call | solution.py:566
  129.0 0.0 copy-start
  129.0 2.8 %copy.9 = bf16[2,512,768]{2,1,0:T(8,128)(2,1)} copy(bf16[2,512,768]{2,1,0:T(8,128)(2,1)} %get-tuple-element.6) | data formatting | bytes 3145728
  131.8 0.0 copy-done
  131.8 0.0 copy-start.1
  131.8 1.1 copy.10
  132.9 0.3 copy-done.1
  133.3 0.8 copy.11
Async XLA Ops:
  129.0 2.8 %copy-start = (bf16[2,64,6144]{2,1,0:T(8,128)(2,1)S(1)}, bf16[2,64,6144]{2,1,0:T(8,128)(2,1)}, u32[]{:S(2)}) copy-start(bf16[2,64,6144]{2,1,0:T(8,128)(2,1)} %get-tuple-element.7) | copy-start | bytes 4718596
  131.8 1.5 %copy-start.1 = (bf16[384,768]{1,0:T(8,128)(2,1)S(1)}, bf16[384,768]{1,0:T(8,128)(2,1)}, u32[]{:S(2)}) copy-start(bf16[384,768]{1,0:T(8,128)(2,1)} %get-tuple-element.8) | copy-start | bytes 1769476

commit v3 on v2

--- a/solution.py
+++ b/solution.py
@@ -21,6 +21,8 @@
 UNIT = 768
 TILE = 256
 FAR, BEFORE, OWN, AFTER = range(4)
+FIRST = [(0, FAR), (1, FAR), (0, BEFORE), (1, AFTER)]
+SECOND = [(1, BEFORE), (0, AFTER), (0, OWN), (1, OWN)]
 
 
 def kernel(
@@ -131,14 +133,14 @@
         part = w_part(v, e_of(rel), cols)
         return remote(part, part, sib_s.at[v, rel], sib_r.at[v, rel], sib)
 
-    def c_rows(s):
-        return c_ref.at[:, at(turn(x, s - OWN) * (2 * ROWS), 2 * ROWS)]
-
-    def c_local(s):
-        return pltpu.make_async_copy(c_rows(s), cg.at[:, s, :, lo], cloc.at[s])
-
-    def c_swap(s, cols):
-        return remote(c_rows(s), cg.at[:, s, :, cols], c_s.at[s], c_r.at[s], zp)
+    def c_rows(m, s):
+        return c_ref.at[m, at(turn(x, s - OWN) * (2 * ROWS), 2 * ROWS)]
+
+    def c_local(m, s):
+        return pltpu.make_async_copy(c_rows(m, s), cg.at[m, s, :, lo], cloc.at[m, s])
+
+    def c_swap(m, s, cols):
+        return remote(c_rows(m, s), cg.at[m, s, :, cols], c_s.at[m, s], c_r.at[m, s], zp)
 
     def dx_ring(v, d, k):
         ks = at(v * UNIT, UNIT)
@@ -188,25 +190,22 @@
         cols = at(off * BLOCK + j * TILE, TILE)
         return jnp.dot(xg[m].reshape(GROUP, HALF), wg[:, cols], preferred_element_type=F32).reshape(4, 2 * ROWS, TILE)
 
-    def dx_rows(v, slots):
-        count = slots.stop - slots.start
-
+    def dx_rows(v, parts):
         @pl.loop(0, UNIT // TILE)
         def _(j):
             ks = at(v * UNIT + j * TILE, TILE)
             acc = lax.dot_general(
-                cg[:, slots].reshape(2 * count * 2 * ROWS, WIDE), wg[ks, :], (((1,), (1,)), ((), ())),
+                jnp.concatenate([cg[m, s] for m, s in parts], axis=0), wg[ks, :], (((1,), (1,)), ((), ())),
                 preferred_element_type=F32,
             )
-            dxp[:, slots, :, ks] = acc.astype(BF16).reshape(2, count, 2 * ROWS, TILE)
-
-    def dx_far(v):
-        dx_rows(v, slice(0, 1))
-
-    def dx_near(v):
-        dx_rows(v, slice(1, 4))
-        for d in (0, 1):
-            dx_ring(v, d, 1).start()
+            for i, (m, s) in enumerate(parts):
+                dxp[m, s, :, ks] = acc[i * 2 * ROWS : (i + 1) * 2 * ROWS].astype(BF16)
+
+    def dx_first(v):
+        dx_rows(v, FIRST)
+        for k in (0, 1):
+            for d in (0, 1):
+                dx_ring(v, d, k).start()
 
     def dx_relay(v):
         ks = at(v * UNIT, UNIT)
@@ -281,8 +280,8 @@
     both = (0, 1)
     for v, e in stripes:
         x_local(v, e).start()
-    for s in range(4):
-        c_local(s).start()
+    for m, s in FIRST + SECOND:
+        c_local(m, s).start()
 
     @pl.when(keeps)
     def _():
@@ -298,10 +297,14 @@
     def _():
         w_diag(lo).start()
 
-    @pl.when(keeps)
-    def _():
-        for v, e in stripes:
-            x_swap(v, e, 0).start()
+    for v, e in stripes:
+        x_swap(v, e, 0).start()
+
+    def c_start():
+        for m, s in FIRST + SECOND:
+            c_swap(m, s, lo).start()
+
+    pl.when(jnp.logical_not(keeps))(c_start)
 
     for v, e in stripes:
         x_local(v, e).wait()
@@ -316,8 +319,6 @@
     @pl.when(jnp.logical_not(keeps))
     def _():
         w_diag(lo).wait_send()
-        for v, e in stripes:
-            x_swap(v, e, 0).start()
         w_diag(lwc).wait_recv()
 
     w_outer(0).start()
@@ -338,22 +339,17 @@
             w_ring(1, d, k).start()
     w_sib(OWN, 1, lwc).start()
     for v, e in stripes:
-        x_swap(v, e, 0).wait_send()
-    c_swap(FAR, lo).start()
-    for v, e in stripes:
         x_swap(v, e, 1).wait_recv()
     for k in both:
         for d in both:
             x_ring(1, d, k).start()
+    pl.when(keeps)(c_start)
     for d in both:
         w_ring(0, d, 1).wait_recv()
         w_sib(before(d), 0, lwc).start()
     for d in both:
         w_ring(0, d, 2).wait_recv()
     w_sib(FAR, 0, lwc).start()
-    c_swap(FAR, lo).wait_send()
-    for s in (AFTER, BEFORE, OWN):
-        c_swap(s, lo).start()
     for d in both:
         w_ring(1, d, 0).wait_recv()
         w_ring(1, d, 2).start()
@@ -368,26 +364,27 @@
         for rel in both:
             w_sib(v, rel, lwz).wait_recv()
 
-    for s in (FAR, AFTER, BEFORE, OWN):
-        c_local(s).wait()
-    c_swap(FAR, lz).wait_recv()
+    for m, s in FIRST + SECOND:
+        c_local(m, s).wait()
+    for m, s in FIRST:
+        c_swap(m, s, lz).wait_recv()
     w_arrived(OWN)
-    dx_far(OWN)
-    for v in (AFTER, BEFORE):
-        w_arrived(v)
-        dx_far(v)
+    w_arrived(AFTER)
+    w_arrived(BEFORE)
+
+    @pl.loop(0, 3)
+    def _(i):
+        dx_first(jnp.where(i == 0, OWN, jnp.where(i == 1, AFTER, BEFORE)))
+
     for d in both:
         w_ring(1, d, 2).wait_recv()
     w_sib(FAR, 1, lwc).start()
     w_arrived(FAR)
-    dx_far(FAR)
+    dx_first(FAR)
     for rel in both:
         for d in both:
             for k in (1, 2):
                 x_ring(rel, d, k).wait_recv()
-    for v in (OWN, AFTER, BEFORE, FAR):
-        for d in both:
-            dx_ring(v, d, 0).start()
 
     def y_first(m):
         @pl.loop(0, BLOCK // TILE)
@@ -396,8 +393,8 @@
 
         y_swap(m).start()
 
+    y_first(0)
     dw_block(FAR, True)
-    y_first(0)
     dw_block(AFTER, True)
 
     @pl.when(keeps)
@@ -425,48 +422,56 @@
     def _():
         dw_merge(OWN)
 
-    for s in (AFTER, BEFORE, OWN):
-        c_swap(s, lz).wait_recv()
-
-    def pick(i, a, b, c_, d_):
-        return jnp.where(i == 0, a, jnp.where(i == 1, b, jnp.where(i == 2, c_, d_)))
-
-    def dx_order(i):
-        return pick(i, OWN, AFTER, BEFORE, FAR)
-
-    def dw_order(i):
-        return pick(i, FAR, AFTER, BEFORE, OWN)
+    for m, s in SECOND:
+        c_swap(m, s, lz).wait_recv()
+    sends = jnp.logical_not(keeps)
+
+    @pl.loop(0, 3)
+    def _(i):
+        dw_block(jnp.where(i == 0, FAR, jnp.where(i == 1, AFTER, BEFORE)), False)
+
+        @pl.when(keeps & (i == 0))
+        def _():
+            for q in both:
+                dw_relay(q)
+
+        @pl.when(sends & (i == 1))
+        def _():
+            dw_merge(FAR)
+            dw_send_far()
+
+        @pl.when(sends & (i == 2))
+        def _():
+            dw_merge(AFTER)
+            dw_send_near(0)
 
     @pl.loop(0, 4)
     def _(i):
-        dw_block(dw_order(i), False)
-        dx_near(dx_order(i))
-
-        @pl.when(jnp.logical_not(keeps))
-        def _():
-            dw_merge(dw_order(i))
-
-            @pl.when(i == 0)
-            def _():
-                dw_send_far()
-
-            @pl.when(i == 1)
-            def _():
-                dw_send_near(0)
-
-            @pl.when(i == 2)
-            def _():
-                dw_send_near(1)
-
-        @pl.when(jnp.where(keeps, 0, 2) == i)
+        v = jnp.where(i == 0, OWN, jnp.where(i == 1, AFTER, jnp.where(i == 2, BEFORE, FAR)))
+
+        @pl.when(i == 3)
+        def _():
+            dw_block(OWN, False)
+
+        dx_rows(v, SECOND)
+
+        @pl.when(sends & (i == 0))
+        def _():
+            dw_merge(BEFORE)
+            dw_send_near(1)
+
+        dx_relay(v)
+
+        @pl.when(sends & (i == 1))
         def _():
             for q in both:
                 dw_relay(q)
 
-        dx_relay(dx_order(i))
-
-    dx_final(OWN)
-    for m in both:
+        @pl.when(sends & (i == 3))
+        def _():
+            dw_merge(OWN)
+
+    def y_second(m):
         y_swap(m).wait_recv()
 
         @pl.loop(0, BLOCK // TILE)
@@ -477,6 +482,7 @@
         for s in range(4):
             y_store(m, s).start()
 
+    dx_final(OWN)
     dx_final(AFTER)
     for q in both:
         for d in both:
@@ -484,8 +490,8 @@
                 dw_ring(d, k, q).wait_recv()
         osnd[:, half(q)] = dw_total(1 - h, q).astype(BF16)
         dw_outer(q).start()
+    y_second(0)
     dx_final(BEFORE)
-    dx_final(FAR)
     for q in both:
         dw_outer(q).wait_recv()
         dwf[:, half(q)] = (dw_total(h, q) + orcv[:, half(q)].astype(F32)).astype(BF16)
@@ -497,6 +503,9 @@
         @pl.when(jnp.logical_not(keeps))
         def _():
             dw_diag(q).start()
+
+    y_second(1)
+    dx_final(FAR)
 
     for q in both:
 
@@ -512,8 +521,10 @@
         for rel in both:
             w_sib(v, rel, lwc).wait_send()
     w_outer(0).wait_send()
-    for s in (AFTER, BEFORE, OWN):
-        c_swap(s, lo).wait_send()
+    for v, e in stripes:
+        x_swap(v, e, 0).wait_send()
+    for m, s in FIRST + SECOND:
+        c_swap(m, s, lo).wait_send()
     for rel in both:
         for d in both:
             for k in range(3):
@@ -539,6 +550,24 @@
             dx_back(v, e, t, False).wait_send()
             dx_back(v, e, 1 - t, False).wait_recv()
             dx_back(v, e, t, True).wait()
+
+
+def hand_on(y_ref, dx_ref, dw_ref, y_out, dx_out, dw_out, y_buf, dx_buf, dw_buf, sem_in, sem_out):
+    pieces = []
+    for m in range(2):
+        for i in range(2):
+            pieces.append((y_ref, y_buf, y_out, (m, pl.ds(i * GROUP // 2, GROUP // 2))))
+        pieces.append((dx_ref, dx_buf, dx_out, (m,)))
+    pieces.append((dw_ref, dw_buf, dw_out, (pl.ds(0, STRIPE),)))
+    loads = [pltpu.make_async_copy(a.at[i], b.at[i], sem_in.at[k]) for k, (a, b, _, i) in enumerate(pieces)]
+    stores = [pltpu.make_async_copy(b.at[i], o.at[i], sem_out.at[k]) for k, (_, b, o, i) in enumerate(pieces)]
+    for load in loads:
+        load.start()
+    for load, store in zip(loads, stores):
+        load.wait()
+        store.start()
+    for store in stores:
+        store.wait()
 
 
 def body(inputs, weight, cotangent):
@@ -554,7 +583,7 @@
         (2, STRIPE, BLOCK), (2, UNIT, BLOCK), (STRIPE, BLOCK), (STRIPE, BLOCK), (STRIPE, BLOCK),
     ]
     sems = [
-        (4, 2), (4, 2), (4, 2), (4,), (4,), (4,), (), (), (), (), (), (2, 2, 3), (2, 2, 3), (2, 2, 3), (2, 2, 3), (4, 2), (4, 2),
+        (4, 2), (4, 2), (4, 2), (2, 4), (2, 4), (2, 4), (), (), (), (), (), (2, 2, 3), (2, 2, 3), (2, 2, 3), (2, 2, 3), (4, 2), (4, 2),
         (4, 2, 3), (4, 2, 3), (4, 2), (4, 2), (4, 2), (2,), (2,), (2, 4), (4,), (4,), (2, 3, 2), (2, 3, 2), (2,), (2,),
         (2,), (2,), (2,),
     ]
@@ -563,7 +592,7 @@
         jax.ShapeDtypeStruct((2, ROWS, 2 * HALF), BF16),
         jax.ShapeDtypeStruct((STRIPE, BLOCK), BF16),
     ]
-    return pl.pallas_call(
+    results = pl.pallas_call(
         functools.partial(kernel, scale),
         out_shape=out,
         in_specs=[pl.BlockSpec(memory_space=pl.ANY)] * 3,
@@ -574,6 +603,14 @@
         ),
         cost_estimate=pl.CostEstimate(flops=29 * 10**9, bytes_accessed=8 * 2**20, transcendentals=0),
     )(inputs, weight, cotangent)
+    return pl.pallas_call(
+        hand_on,
+        out_shape=out,
+        in_specs=[pl.BlockSpec(memory_space=pl.ANY)] * 3,
+        out_specs=[pl.BlockSpec(memory_space=pl.ANY)] * 3,
+        scratch_shapes=[pltpu.VMEM(o.shape, BF16) for o in out] + [dma((7,)), dma((7,))],
+        compiler_params=pltpu.CompilerParams(vmem_limit_bytes=62 * 2**20),
+    )(*results)
 
 
 def solution(mesh):

time: 134 us -> 133 us (level)
  local copies, waits for them, and re-layouts: 5.05 us -> 0 us
  Pallas kernels: 128 us -> 132 us
    unnamed x7 -> x0, local copies, waits for them, and re-layouts: 5.05 us -> none
    pallas_call x0 -> x1, Pallas kernels: none -> 3.24 us  [body(): pl.pallas_call(hand_on, out_shape=out, in_specs=[pl.BlockSpec(memory_spac...]
where the time goes in v3:
time: 133 us
  Pallas kernels  132 us (99%)
    pallas_call x1, Pallas kernels, body(): pl.pallas_call(functools.partial(kernel, scale), out_shape=out, in_specs=...  129 us
    pallas_call x1, Pallas kernels, body(): pl.pallas_call(hand_on, out_shape=out, in_specs=[pl.BlockSpec(memory_spac...  3.24 us

profile of v3, /device:TPU:1, one launch (start us, length us, event | category | flops | bytes accessed | tf_op | source)
XLA Modules:
  0.0 132.5 jit_solution(11516301712866950423)
XLA Ops:
  0.6 128.7 %shard_map.58 = (bf16[2,512,768]{2,1,0:T(8,128)(2,1)}, bf16[2,64,6144]{2,1,0:T(8,128)(2,1)}, bf16[384,768]{1,0:T(8,128)(2,1)}) custom-call(bf16[2,64,6144]{2,1,0:T(8,128)(2,1)} %x_ref.1, bf16[384,768]{1,0:T(8,128)(2,1)} %w_ref.1, bf16[2,512,768]{2,1,0:T(8,128)(2,1)} %c_ref.1), custom_call_target="tpu_custom_call" | custom-call | flops 28999999488 | bytes 8388608 | tf_op jit(solution)/shard_map/pallas_call | solution.py:595
  129.3 3.2 %shard_map.59 = (bf16[2,512,768]{2,1,0:T(8,128)(2,1)}, bf16[2,64,6144]{2,1,0:T(8,128)(2,1)}, bf16[384,768]{1,0:T(8,128)(2,1)}) custom-call(bf16[2,512,768]{2,1,0:T(8,128)(2,1)} %get-tuple-element.6.y_ref, bf16[2,64,6144]{2,1,0:T(8,128)(2,1)} %get-tuple-element.7.dx_ref, bf16[384,768]{1,0:T(8,128)(2,1)} %get-tuple-element.8.dw_ref), custom_call_target="tpu_custom_call" | custom-call | tf_op jit(solution)/shard_map/pallas_call | solution.py:606

commit v4 on v3

--- a/solution.py
+++ b/solution.py
@@ -61,6 +61,9 @@
     def at(start, size):
         return pl.ds(pl.multiple_of(start, size), size)
 
+    def third(q):
+        return slice(q * TILE, (q + 1) * TILE)
+
     def half(q):
         return slice(q * STRIPE, (q + 1) * STRIPE)
 
@@ -173,18 +176,18 @@
 
     def dw_ring(d, k, q):
         p = piece(d, k)
-        src = dwp.at[0, dw_rows(FAR if k == 0 else ahead(d), p), half(q)]
-        dst = fy.at[d, :, half(q)] if k == 0 else ny.at[d, half(p), half(q)]
+        src = dwp.at[0, dw_rows(FAR if k == 0 else ahead(d), p), third(q)]
+        dst = fy.at[d, :, third(q)] if k == 0 else ny.at[d, half(p), third(q)]
         return remote(src, dst, dy_s.at[d, k, q], dy_r.at[d, k, q], yn[d])
 
     def dw_outer(q):
-        return remote(osnd.at[:, half(q)], orcv.at[:, half(q)], do_s.at[q], do_r.at[q], outer)
+        return remote(osnd.at[:, third(q)], orcv.at[:, third(q)], do_s.at[q], do_r.at[q], outer)
 
     def dw_diag(q):
-        return remote(dwf.at[:, half(q)], dw_out.at[:, half(q)], dd_s.at[q], dd_r.at[q], diag)
+        return remote(dwf.at[:, third(q)], dw_out.at[:, third(q)], dd_s.at[q], dd_r.at[q], diag)
 
     def dw_local(q):
-        return pltpu.make_async_copy(dwf.at[:, half(q)], dw_out.at[:, half(q)], ddl.at[q])
+        return pltpu.make_async_copy(dwf.at[:, third(q)], dw_out.at[:, third(q)], ddl.at[q])
 
     def y_tile(m, off, j):
         cols = at(off * BLOCK + j * TILE, TILE)
@@ -253,27 +256,27 @@
             dwp[0, part, :] = (dwp[0, part, :].astype(F32) + dwr[part, :].astype(F32)).astype(BF16)
 
     def dw_send_far():
-        for q in (0, 1):
+        for q in range(3):
             for d in (0, 1):
                 dw_ring(d, 0, q).start()
 
     def dw_send_near(d):
-        for q in (0, 1):
+        for q in range(3):
             dw_ring(d, 1, q).start()
 
     def dw_relay(q):
         for d in (0, 1):
             dw_ring(d, 0, q).wait_recv()
             rows = dw_rows(ahead(d), d)
-            dwp[0, rows, half(q)] = (dwp[0, rows, half(q)].astype(F32) + fy[d, :, half(q)].astype(F32)).astype(BF16)
+            dwp[0, rows, third(q)] = (dwp[0, rows, third(q)].astype(F32) + fy[d, :, third(q)].astype(F32)).astype(BF16)
             dw_ring(d, 2, q).start()
 
     def dw_total(e, q):
         rows = at(e * STRIPE, STRIPE)
         return (
-            dwp[0, dw_rows(OWN, e), half(q)].astype(F32)
-            + ny[0, rows, half(q)].astype(F32)
-            + ny[1, rows, half(q)].astype(F32)
+            dwp[0, dw_rows(OWN, e), third(q)].astype(F32)
+            + ny[0, rows, third(q)].astype(F32)
+            + ny[1, rows, third(q)].astype(F32)
         )
 
     stripes = [(v, e) for v in range(4) for e in range(2)]
@@ -432,7 +435,7 @@
 
         @pl.when(keeps & (i == 0))
         def _():
-            for q in both:
+            for q in range(3):
                 dw_relay(q)
 
         @pl.when(sends & (i == 1))
@@ -464,7 +467,7 @@
 
         @pl.when(sends & (i == 1))
         def _():
-            for q in both:
+            for q in range(3):
                 dw_relay(q)
 
         @pl.when(sends & (i == 3))
@@ -484,17 +487,18 @@
 
     dx_final(OWN)
     dx_final(AFTER)
-    for q in both:
+    for q in range(3):
         for d in both:
             for k in (1, 2):
                 dw_ring(d, k, q).wait_recv()
-        osnd[:, half(q)] = dw_total(1 - h, q).astype(BF16)
+        osnd[:, third(q)] = dw_total(1 - h, q).astype(BF16)
         dw_outer(q).start()
+    dx_final(BEFORE)
     y_second(0)
-    dx_final(BEFORE)
-    for q in both:
+    dx_final(FAR)
+    for q in range(3):
         dw_outer(q).wait_recv()
-        dwf[:, half(q)] = (dw_total(h, q) + orcv[:, half(q)].astype(F32)).astype(BF16)
+        dwf[:, third(q)] = (dw_total(h, q) + orcv[:, third(q)].astype(F32)).astype(BF16)
 
         @pl.when(keeps)
         def _():
@@ -505,9 +509,8 @@
             dw_diag(q).start()
 
     y_second(1)
-    dx_final(FAR)
-
-    for q in both:
+
+    for q in range(3):
 
         @pl.when(keeps)
         def _():
@@ -530,7 +533,7 @@
             for k in range(3):
                 x_ring(rel, d, k).wait_send()
                 w_ring(rel, d, k).wait_send()
-    for q in both:
+    for q in range(3):
         for d in both:
             for k in range(3):
                 dw_ring(d, k, q).wait_send()
@@ -584,8 +587,8 @@
     ]
     sems = [
         (4, 2), (4, 2), (4, 2), (2, 4), (2, 4), (2, 4), (), (), (), (), (), (2, 2, 3), (2, 2, 3), (2, 2, 3), (2, 2, 3), (4, 2), (4, 2),
-        (4, 2, 3), (4, 2, 3), (4, 2), (4, 2), (4, 2), (2,), (2,), (2, 4), (4,), (4,), (2, 3, 2), (2, 3, 2), (2,), (2,),
-        (2,), (2,), (2,),
+        (4, 2, 3), (4, 2, 3), (4, 2), (4, 2), (4, 2), (2,), (2,), (2, 4), (4,), (4,), (2, 3, 3), (2, 3, 3), (3,), (3,),
+        (3,), (3,), (3,),
     ]
     out = [
         jax.ShapeDtypeStruct((2, GROUP, BLOCK), BF16),

time: 133 us -> 131 us (0.985)
  Pallas kernels: 132 us -> 130 us
    pallas_call x1, Pallas kernels: 129 us -> 127 us  [body(): pl.pallas_call(functools.partial(kernel, scale), out_shape=out, in_specs=...]
where the time goes in v4:
time: 131 us
  Pallas kernels  130 us (99%)
    pallas_call x1, Pallas kernels, body(): pl.pallas_call(functools.partial(kernel, scale), out_shape=out, in_specs=...  127 us
    pallas_call x1, Pallas kernels, body(): pl.pallas_call(hand_on, out_shape=out, in_specs=[pl.BlockSpec(memory_spac...  3.24 us

profile of v4, /device:TPU:1, one launch (start us, length us, event | category | flops | bytes accessed | tf_op | source)
XLA Modules:
  0.0 130.7 jit_solution(3465444458657197461)
XLA Ops:
  0.6 126.8 %shard_map.58 = (bf16[2,512,768]{2,1,0:T(8,128)(2,1)}, bf16[2,64,6144]{2,1,0:T(8,128)(2,1)}, bf16[384,768]{1,0:T(8,128)(2,1)}) custom-call(bf16[2,64,6144]{2,1,0:T(8,128)(2,1)} %x_ref.1, bf16[384,768]{1,0:T(8,128)(2,1)} %w_ref.1, bf16[2,512,768]{2,1,0:T(8,128)(2,1)} %c_ref.1), custom_call_target="tpu_custom_call" | custom-call | flops 28999999488 | bytes 8388608 | tf_op jit(solution)/shard_map/pallas_call | solution.py:598
  127.5 3.2 %shard_map.59 = (bf16[2,512,768]{2,1,0:T(8,128)(2,1)}, bf16[2,64,6144]{2,1,0:T(8,128)(2,1)}, bf16[384,768]{1,0:T(8,128)(2,1)}) custom-call(bf16[2,512,768]{2,1,0:T(8,128)(2,1)} %get-tuple-element.6.y_ref, bf16[2,64,6144]{2,1,0:T(8,128)(2,1)} %get-tuple-element.7.dx_ref, bf16[384,768]{1,0:T(8,128)(2,1)} %get-tuple-element.8.dw_ref), custom_call_target="tpu_custom_call" | custom-call | tf_op jit(solution)/shard_map/pallas_call | solution.py:609

commit v5 on v4

--- a/solution.py
+++ b/solution.py
@@ -494,7 +494,6 @@
         osnd[:, third(q)] = dw_total(1 - h, q).astype(BF16)
         dw_outer(q).start()
     dx_final(BEFORE)
-    y_second(0)
     dx_final(FAR)
     for q in range(3):
         dw_outer(q).wait_recv()
@@ -508,6 +507,7 @@
         def _():
             dw_diag(q).start()
 
+    y_second(0)
     y_second(1)
 
     for q in range(3):

time: 131 us -> 132 us (level)
  no operation moved by 1% of the time
where the time goes in v5:
time: 132 us; the launch traced here: 131 us
  Pallas kernels  130 us (98%)
    pallas_call x1, Pallas kernels, body(): pl.pallas_call(functools.partial(kernel, scale), out_shape=out, in_specs=...  127 us
    pallas_call x1, Pallas kernels, body(): pl.pallas_call(hand_on, out_shape=out, in_specs=[pl.BlockSpec(memory_spac...  3.24 us

profile of v5, /device:TPU:1, one launch (start us, length us, event | category | flops | bytes accessed | tf_op | source)
XLA Modules:
  0.0 130.9 jit_solution(3333478302324518218)
XLA Ops:
  0.6 127.0 %shard_map.58 = (bf16[2,512,768]{2,1,0:T(8,128)(2,1)}, bf16[2,64,6144]{2,1,0:T(8,128)(2,1)}, bf16[384,768]{1,0:T(8,128)(2,1)}) custom-call(bf16[2,64,6144]{2,1,0:T(8,128)(2,1)} %x_ref.1, bf16[384,768]{1,0:T(8,128)(2,1)} %w_ref.1, bf16[2,512,768]{2,1,0:T(8,128)(2,1)} %c_ref.1), custom_call_target="tpu_custom_call" | custom-call | flops 28999999488 | bytes 8388608 | tf_op jit(solution)/shard_map/pallas_call | solution.py:598
  127.7 3.2 %shard_map.59 = (bf16[2,512,768]{2,1,0:T(8,128)(2,1)}, bf16[2,64,6144]{2,1,0:T(8,128)(2,1)}, bf16[384,768]{1,0:T(8,128)(2,1)}) custom-call(bf16[2,512,768]{2,1,0:T(8,128)(2,1)} %get-tuple-element.6.y_ref, bf16[2,64,6144]{2,1,0:T(8,128)(2,1)} %get-tuple-element.7.dx_ref, bf16[384,768]{1,0:T(8,128)(2,1)} %get-tuple-element.8.dw_ref), custom_call_target="tpu_custom_call" | custom-call | tf_op jit(solution)/shard_map/pallas_call | solution.py:609
